TPU v7x, 512 devices: a whole 4x4x16 slice. The times are simulated.
512 devices in a mesh: tensor: 8 (over y, core), vocab: 64 (over z, x).
Axes of the slice: x: 4, y: 4, z: 16, core: 2. Of those that a mesh axis runs over, the one named last changes fastest.
Arguments:
- partials: bfloat16 [3, 8, 256, 4096], P(None, 'tensor', 'vocab'), may hold values from -256 to 256
- norm_gain: bfloat16 [4096], replicated, may hold values from 0.5 to 1.5
- head_weight: bfloat16 [4096, 131072], P(None, ('tensor', 'vocab')), may hold values from -0.7861328 to 0.7861328
- draft_ids: int32 [3, 256], replicated, may hold values from 0 to 131071
- tree_parents: int32 [256], replicated, may hold values from 0 to 62, as said below
- accepted_lengths: int32 [3, 4], replicated, may hold values from 1 to 5
Outputs:
- probabilities: bfloat16 [3, 256, 131072], P(None, None, ('tensor', 'vocab'))
- entropy: float32 [3, 256], replicated
- typical_margin: float32 [3, 256], replicated
- path_score: float32 [3, 4], replicated
Inputs may be any that keep to these rules, and one draw needn't show every extreme that they name: `tree_parents`: each row names an earlier row of its own tree of 64 rows by its position in the tree; a tree's first row names itself.
All inputs are finite; a program needn't handle non-finite values.
Results may differ from a plain program's by a relative error of at most 0.009.
Values may be sent and summed in bfloat16 or wider, within the bound.
A program may use at most 64 MiB of HBM per device.

v0:
```python
import math

import jax
import jax.numpy as jnp
from jax import lax
from jax.sharding import PartitionSpec as P

HBLOCK = 128
NODES = 64
ROUNDS = 3


norm_eps = 1e-06
typical_alpha = 0.3


def hadamard_table(size):
    index = jnp.arange(size, dtype=jnp.int32)
    common = index[:, None] & index[None, :]
    parity = jnp.zeros((size, size), jnp.int32)
    for shift_bit in range(max(size.bit_length(), 1)):
        parity = parity + (jnp.right_shift(common, shift_bit) & 1)
    signs = (1 - 2 * (parity % 2)).astype(jnp.float32)
    return signs / jnp.sqrt(jnp.float32(size))


def rotate_blocks(normed, table):
    count, width = normed.shape
    block = table.shape[0]
    blocks = normed.reshape(count, width // block, block)
    turned = jnp.einsum("rbk,kj->rbj", blocks, table, precision=lax.Precision.HIGHEST)
    return turned.reshape(count, width).astype(jnp.bfloat16)


def tree_depth(tree_parents):
    parents = tree_parents.reshape(-1, NODES)
    depth = jnp.broadcast_to((jnp.arange(NODES) > 0).astype(jnp.int32), parents.shape)
    for jump in range(NODES.bit_length()):
        depth = depth + jnp.take_along_axis(depth, parents, axis=1)
        parents = jnp.take_along_axis(parents, parents, axis=1)
    return depth


def body(partials, norm_gain, head_weight, draft_ids, tree_parents, accepted_lengths):
    table = hadamard_table(HBLOCK)
    depth = tree_depth(tree_parents)
    rows_total = draft_ids.shape[1]
    vocab_width = head_weight.shape[1]
    vocab_start = (
        lax.axis_index("tensor") * lax.axis_size("vocab") + lax.axis_index("vocab")
    ) * vocab_width
    row_index = jnp.arange(rows_total, dtype=jnp.int32)
    parent_row = row_index // NODES * NODES + tree_parents
    gain = norm_gain.astype(jnp.float32)
    prob_list = []
    entropy_list = []
    margin_list = []
    score_list = []
    for round_index in range(ROUNDS):
        piece = partials[round_index, 0].astype(jnp.float32)
        logits = None
        full_rows = None
        hidden = lax.psum(piece, "tensor")
        mean_square = jnp.mean(hidden * hidden, axis=1, keepdims=True)
        full_rows = rotate_blocks(hidden * lax.rsqrt(mean_square + norm_eps) * gain, table)
        logits = jnp.dot(
            lax.all_gather(full_rows, "vocab", axis=0, tiled=True),
            head_weight,
            preferred_element_type=jnp.float32,
        )
        local_max = jnp.max(logits, axis=1)
        shifted = logits - local_max[:, None]
        weights = jnp.exp(shifted)
        local_total = jnp.sum(weights, axis=1)
        local_spread = jnp.sum(weights * shifted, axis=1)
        column = draft_ids[round_index] - vocab_start
        inside = (column >= 0) & (column < vocab_width)
        flat_index = parent_row * vocab_width + jnp.clip(column, 0, vocab_width - 1)
        local_pick = jnp.where(inside, logits.reshape(-1)[flat_index], jnp.float32(0.0))
        row_max = lax.pmax(local_max, ("tensor", "vocab"))
        rescale = jnp.exp(local_max - row_max)
        totals, spread, picked = lax.psum(
            (
                local_total * rescale,
                rescale * (local_spread + (local_max - row_max) * local_total),
                local_pick,
            ),
            ("tensor", "vocab"),
        )
        prob_list.append((weights * (rescale / totals)[:, None]).astype(jnp.bfloat16))
        entropy = jnp.log(totals) - spread / totals
        log_draft = picked - row_max[parent_row] - jnp.log(totals[parent_row])
        margin = log_draft + entropy[parent_row] - math.log(typical_alpha)
        survive = depth < accepted_lengths[round_index][:, None]
        chosen = jnp.where(survive, log_draft.reshape(-1, NODES), jnp.float32(0.0))
        counted = jnp.sum(survive.astype(jnp.float32), axis=1)
        score = jnp.sum(chosen, axis=1) / counted
        entropy_list.append(entropy)
        margin_list.append(margin)
        score_list.append(score)
    return (
        jnp.stack(prob_list),
        jnp.stack(entropy_list),
        jnp.stack(margin_list),
        jnp.stack(score_list),
    )


def solution(mesh):
    placed = (P(None, "tensor", "vocab", None), P(), P(None, ("tensor", "vocab")), P(), P(), P())
    return jax.shard_map(
        body,
        mesh=mesh,
        in_specs=placed,
        out_specs=(P(None, None, ("tensor", "vocab")), P(), P(), P()),
        check_vma=False,
    )
```

profile of v0, /device:TPU:1, one launch (start us, length us, event | category | flops | bytes accessed | tf_op | source)
XLA Modules:
  0.0 760.2 jit_solution(2659814930392972517)
XLA Ops:
  7.2 1.6 bitcast_convert_fusion.2
  8.9 0.7 convert_element_type.71
  9.6 80.7 %all-reduce.5.cloned.1.call-done = (f32[4,4096]{1,0:T(4,128)}, f32[4,4096]{1,0:T(4,128)}, f32[4,4096]{1,0:T(4,128)}) async-done(((f32[4,4096]{1,0:T(4,128)}, f32[4,4096]{1,0:T(4,128)}, f32[4,4096]{1,0:T(4,128)}), (f32[4,4096]{1,0:T(4,128)}, f32[4,4096]{1,0:T(4,128)}, f32[4,4096]{1,0:T(4,128)})) %all-reduce.5.cloned.1.call-update) | async-done | bytes 196624 | tf_op jit(solution)/shard_map/psum | solution.py:63
  90.3 1.0 multiply_reduce_fusion.2
  91.3 1.1 multiply_reduce_fusion
  92.4 1.0 multiply_bitcast_fusion.2
  94.7 0.6 reshape.436
  95.6 2.4 gather_fusion.13
  98.0 2.4 gather_fusion.12
  100.7 2.4 gather_fusion.14
  103.3 2.4 gather_fusion.15
  105.9 2.4 gather_fusion.16
  108.4 2.4 gather_fusion.17
  112.0 2.4 gather_fusion.18
  114.5 2.4 gather_fusion.19
  117.1 2.4 gather_fusion.20
  119.6 2.4 gather_fusion.21
  122.2 2.4 gather_fusion.23
  124.8 2.4 gather_fusion.22
  127.4 2.4 gather_fusion.24
  130.2 97.0 %all-gather.11.cloned.1.call-done = bf16[64,4,4096]{2,1,0:T(4,128)(2,1)} async-done(((bf16[1,4,4096]{2,1,0:T(4,128)(2,1)}), bf16[64,4,4096]{2,1,0:T(4,128)(2,1)}) %all-gather.11.cloned.1.call-update) | async-done | bytes 2097168 | tf_op jit(solution)/shard_map/all_gather | solution.py:67
  227.2 4.0 reshape.439
  231.2 2.5 fusion.81
  233.8 133.7 %all-gather.9.cloned.1.call-done = bf16[64,4,4096]{2,1,0:T(4,128)(2,1)} async-done(((bf16[1,4,4096]{2,1,0:T(4,128)(2,1)}), bf16[64,4,4096]{2,1,0:T(4,128)(2,1)}) %all-gather.9.cloned.1.call-update) | async-done | bytes 2097168 | tf_op jit(solution)/shard_map/all_gather | solution.py:67
  367.5 4.0 reshape.437
  371.6 2.5 fusion.82
  374.1 133.6 %all-gather.7.cloned.1.call-done = bf16[64,4,4096]{2,1,0:T(4,128)(2,1)} async-done(((bf16[1,4,4096]{2,1,0:T(4,128)(2,1)}), bf16[64,4,4096]{2,1,0:T(4,128)(2,1)}) %all-gather.7.cloned.1.call-update) | async-done | bytes 2097168 | tf_op jit(solution)/shard_map/all_gather | solution.py:67
  507.7 4.0 reshape.435
  511.7 2.5 fusion.83
  514.2 0.8 copy.16
  515.2 109.7 %all-reduce.1 = (f32[256]{0:T(256)S(1)}, f32[256]{0:T(256)S(1)}, f32[256]{0:T(256)S(1)}) all-reduce(f32[256]{0:T(256)S(1)} %get-tuple-element.98, f32[256]{0:T(256)S(1)} %get-tuple-element.100, f32[256]{0:T(256)S(1)} %get-tuple-element.102), channel_id=1, replica_groups=mesh['tensor'=8,'vocab'=64] {'tensor','vocab'}, use_global_device_ids=true, to_apply=%region_15.16 | all-reduce | flops 768 | bytes 6144 | tf_op jit(solution)/shard_map/pmax | solution.py:80
  624.9 0.8 copy.15
  625.9 1.1 copy.23
  626.9 1.1 copy.22
  628.0 1.9 gather_fusion.9
  630.0 1.9 gather_fusion.5
  631.9 1.9 gather_fusion.1
  633.9 1.7 gather_fusion.8
  635.7 1.7 gather_fusion.4
  637.4 1.7 gather_fusion
  639.2 99.0 %all-reduce = (f32[256]{0:T(256)S(1)}, f32[256]{0:T(256)S(1)}, f32[256]{0:T(256)S(1)}, f32[256]{0:T(256)S(1)}, f32[256]{0:T(256)S(1)}, /*index=5*/f32[256]{0:T(2...) all-reduce(f32[256]{0:T(256)S(1)} %get-tuple-element.83, ...), channel_id=1, replica_groups=mesh['tensor'=8,'vocab'=64] {'tensor','vocab'}, use_global_device_ids=true, to_apply=%region_17.18 | all-reduce | flops 2304 | bytes 18432 | tf_op jit(solution)/shard_map/psum | solution.py:82
  738.2 1.9 gather_fusion.10
  740.2 1.9 gather_fusion.6
  742.3 1.9 gather_fusion.2
  744.3 0.9 copy.18
  745.3 1.9 gather_fusion.11
  747.2 1.9 gather_fusion.7
  749.2 1.9 gather_fusion.3
  (107 shorter events, 7.8 us)
Async XLA Ops:
  7.2 224.0 %copy-start = (bf16[4096,256]{1,0:T(8,128)(2,1)S(1)}, bf16[4096,256]{1,0:T(8,128)(2,1)}, u32[]{:S(2)}) copy-start(bf16[4096,256]{1,0:T(8,128)(2,1)} %param.10) | copy-start | bytes 6291460
  7.2 88.2 %copy-start.4 = (s32[256]{0:T(256)S(1)}, s32[256]{0:T(256)}, u32[]{:S(2)}) copy-start(s32[256]{0:T(256)} %param.12) | copy-start | bytes 3076
  7.2 83.1 %all-reduce.5.cloned.1.call-start = ((), (), s32[]{:S(2)}) async-start(), calls=%async_computation.3 | async-start | bytes 393216 | tf_op jit(solution)/shard_map/psum | solution.py:63
  8.9 218.3 %all-gather.11.cloned.1.call-start = ((), (), s32[]{:S(2)}) async-start(), calls=%async_computation.2 | async-start | bytes 2129920 | tf_op jit(solution)/shard_map/all_gather | solution.py:67
  94.3 273.2 %all-gather.9.cloned.1.call-start = ((), (), s32[]{:S(2)}) async-start(), calls=%async_computation.1 | async-start | bytes 2129920 | tf_op jit(solution)/shard_map/all_gather | solution.py:67
  95.3 412.4 %all-gather.7.cloned.1.call-start = ((), (), s32[]{:S(2)}) async-start(), calls=%async_computation | async-start | bytes 2129920 | tf_op jit(solution)/shard_map/all_gather | solution.py:67
  124.8 5.2 copy-start.3
  124.8 5.3 copy-start.5
  374.1 141.0 %copy-start.1 = (f32[256,256]{0,1:T(8,128)}, f32[256,256]{0,1:T(8,128)S(1)}, u32[]{:S(2)}) copy-start(f32[256,256]{0,1:T(8,128)S(1)} %get-tuple-element.101) | copy-start | bytes 786436
  635.7 106.5 %copy-start.2 = (f32[256,256]{0,1:T(8,128)S(1)}, f32[256,256]{0,1:T(8,128)}, u32[]{:S(2)}) copy-start(f32[256,256]{0,1:T(8,128)} %copy-done.1) | copy-start | bytes 786436
Sparse Core Ops, SparseCore 0:
  11.1 79.1 all-reduce.4
  94.4 132.6 all-gather.10
  230.6 136.9 all-gather.8
  370.8 136.9 all-gather.6
where the time goes:
time: 761 us; the launch traced here: 760 us
  waiting for transfers between devices  445 us (58%)
  blocking collectives  209 us (27%)
  local copies, waits for them, and re-layouts  75.1 us (10%)
  between operations  14.3 us (2%)
  other arithmetic  8.51 us (1%)
  matrix products  8.45 us (1%)
    all_gather x3, waiting for transfers between devices, body(): lax.all_gather(full_rows, 'vocab', axis=0, tiled=True)  364 us
    pmax x1, blocking collectives, body(): row_max = lax.pmax(local_max, ('tensor', 'vocab'))  110 us
    psum x1, blocking collectives, body(): lax.psum((local_total * rescale, rescale * (local_spread + (local_max - r...  99 us
    psum x1, waiting for transfers between devices, body(): hidden = lax.psum(piece, 'tensor')  80.7 us
    gather x21, local copies, waits for them, and re-layouts, tree_depth(): depth = depth + jnp.take_along_axis(depth, parents, axis=1)  18.2 us
    unnamed x22, local copies, waits for them, and re-layouts  17.1 us
  transfers between devices with their start and end apart: 4, of which 4 were waited for; matrix products, arithmetic and copies ran while one was open for 6% of the time, Pallas kernels for 0%

commit v1 on v0

v1 whole, which is shorter than its diff:
```python
import math

import jax
import jax.numpy as jnp
from jax import lax
from jax.experimental import pallas as pl
from jax.experimental.pallas import tpu as pltpu
from jax.sharding import PartitionSpec as P

MESH = pl.DeviceIdType.MESH
HIGHEST = lax.Precision.HIGHEST
F32 = jnp.float32
BF16 = jnp.bfloat16

X = 4
Y = 4
Z = 16
PLANE = 32
KHALF = 2048
COLS = 256
ROUNDS = 3
NODES = 64
norm_eps = 1e-06
typical_alpha = 0.3


def dot(a, b, precision=None):
    return jnp.dot(a, b, precision=precision, preferred_element_type=F32)


def iota(shape, dim):
    return lax.broadcasted_iota(jnp.int32, shape, dim)


def kernel(
    partials,
    gain,
    weight,
    draft,
    parents,
    accepted,
    prob,
    entropy_out,
    margin_out,
    score_out,
    wbuf,
    rs_send,
    rs_recv,
    ss_send,
    ss_recv,
    xg,
    lp,
    lr,
    lf,
    quant,
    st_send,
    st_plane,
    st_mid,
    st_z,
    st_own,
    st_sib,
    psend,
    w_sem,
    rs_sem,
    ss_sem,
    z_sem,
    zs_sem,
    p1_sem,
    p1s_sem,
    p2_sem,
    p2s_sem,
    l_sem,
    ls_sem,
    sp_sem,
    sz_sem,
    sb_sem,
    pr_sem,
):
    t = lax.axis_index("tensor")
    v = lax.axis_index("vocab")
    x = lax.rem(v, X)
    z = lax.div(v, X)
    y = lax.div(t, 2)
    c = lax.rem(t, 2)
    sib = 1 - c

    def dev(dx, dy, dz, dc):
        return (dy * 2 + dc, dz * X + dx)

    def wait(ref, sem):
        pltpu.make_async_copy(ref, ref, sem).wait()

    def send(src, dst, ssem, rsem, device):
        pltpu.make_async_remote_copy(
            src_ref=src,
            dst_ref=dst,
            send_sem=ssem,
            recv_sem=rsem,
            device_id=device,
            device_id_type=MESH,
        ).start()

    me = c * 16 + x * Y + y

    def plane_dev(j):
        return dev(lax.div(lax.rem(j, 16), Y), lax.rem(j, Y), z, lax.div(j, 16))

    def offset(k):
        half = lax.div(k + 1, 2)
        return lax.rem(k, 2) * 2 * half - half

    def zmate(o):
        return lax.rem(z + o + Z, Z)

    barrier = pltpu.get_barrier_semaphore()

    def greet_plane(i, carry):
        j = lax.rem(me + i, PLANE)
        pl.semaphore_signal(barrier, inc=1, device_id=plane_dev(j), device_id_type=MESH)
        return carry

    def greet_z(i, carry):
        pl.semaphore_signal(
            barrier, inc=1, device_id=dev(x, y, zmate(i), c), device_id_type=MESH
        )
        return carry

    lax.fori_loop(1, PLANE, greet_plane, 0)
    lax.fori_loop(1, Z, greet_z, 0)

    own_w = pltpu.make_async_copy(
        weight.at[pl.ds(c * KHALF, KHALF)], wbuf.at[c], w_sem.at[0]
    )
    own_w.start()

    rows = [partials[r, 0].astype(F32) for r in range(ROUNDS)]
    slab = jnp.concatenate(rows + [jnp.zeros_like(rows[0])], axis=0).astype(BF16)
    for j in range(PLANE):
        rs_send[j] = slab[:, j * 128 : (j + 1) * 128]

    pl.semaphore_wait(barrier, PLANE - 1 + Z - 1)

    def rs_start(i, carry):
        j = lax.rem(me + i, PLANE)
        send(rs_send.at[j], rs_recv.at[me], rs_sem.at[0], rs_sem.at[1], plane_dev(j))
        return carry

    lax.fori_loop(1, PLANE, rs_start, 0)
    rs_recv[me] = rs_send[me]

    swap_w = pltpu.make_async_remote_copy(
        src_ref=weight.at[pl.ds(sib * KHALF, KHALF)],
        dst_ref=wbuf.at[c],
        send_sem=w_sem.at[1],
        recv_sem=w_sem.at[2],
        device_id=dev(x, y, z, sib),
        device_id_type=MESH,
    )

    common = iota((128, 128), 0) & iota((128, 128), 1)
    parity = jnp.zeros((128, 128), jnp.int32)
    for bit in range(7):
        parity = parity + (lax.shift_right_logical(common, bit) & 1)
    signs = (1 - 2 * (parity & 1)).astype(F32)

    parent_row = lax.div(iota((1, 256), 1), NODES) * NODES + parents[...]
    jump = (iota((256, 256), 0) == parent_row).astype(BF16)
    depth = jnp.broadcast_to(
        (lax.rem(iota((1, 256), 1), NODES) > 0).astype(F32), (8, 256)
    )
    for step in range(NODES.bit_length()):
        depth = depth + dot(depth.astype(BF16), jump)
        if step < NODES.bit_length() - 1:
            jump = dot(jump, jump).astype(BF16)

    gain_row = gain[me]

    wait(rs_recv.at[pl.ds(0, PLANE - 1)], rs_sem.at[1])
    swap_w.start()

    pieces = []
    for dx in range(X):
        total = jnp.zeros((16, 128), F32)
        for dy in range(Y):
            for dc in range(2):
                total = total + rs_recv[dc * 16 + dx * Y + dy].astype(F32)
        pieces.append(total)
    hidden = jnp.concatenate(
        [pieces[dx][4 * r : 4 * r + 4] for r in range(ROUNDS) for dx in range(X)],
        axis=0,
    )
    square = jnp.concatenate([hidden * hidden, jnp.zeros((80, 128), F32)], axis=0)
    ss_send[...] = jnp.broadcast_to(
        jnp.sum(square.T, axis=0, keepdims=True), (8, 128)
    )

    def ss_start(i, carry):
        j = lax.rem(me + i, PLANE)
        send(ss_send, ss_recv.at[me], ss_sem.at[0], ss_sem.at[1], plane_dev(j))
        return carry

    lax.fori_loop(1, PLANE, ss_start, 0)
    ss_recv[me] = ss_send[...]
    wait(ss_recv.at[pl.ds(0, PLANE - 1)], ss_sem.at[1])
    sums = ss_recv[0]
    for j in range(1, PLANE):
        sums = sums + ss_recv[j]
    scale = lax.rsqrt(sums[0:1] * (1.0 / 4096.0) + norm_eps)
    scale = jnp.broadcast_to(scale, (128, 128)).T[0:48]
    normed = hidden * scale * gain_row
    rotated = dot(normed, signs, HIGHEST) * (1.0 / math.sqrt(128.0))
    xg[x, y, z] = rotated.astype(BF16)

    def z_start(k, carry):
        send(
            xg.at[x, y, z],
            xg.at[x, y, z],
            zs_sem.at[0],
            z_sem.at[k],
            dev(x, y, zmate(-offset(k)), c),
        )
        return carry

    def across(k, order):
        zs = zmate(offset(k))
        chunk = xg.at[x, y, zs]

        def step(i, carry):
            target = (
                dev(lax.rem(x + i, X), y, z, c)
                if order == 0
                else dev(x, lax.rem(y + i, Y), z, c)
            )
            send(chunk, chunk, p1s_sem.at[0], p1_sem.at[k], target)
            return carry

        lax.fori_loop(1, 4, step, 0)

    def along(k, order):
        zs = zmate(offset(k))
        wait(xg.at[0, pl.ds(0, 3), 0], p1_sem.at[k])
        line = xg.at[:, y, zs] if order == 0 else xg.at[x, :, zs]

        def step(i, carry):
            target = (
                dev(x, lax.rem(y + i, Y), z, c)
                if order == 0
                else dev(lax.rem(x + i, X), y, z, c)
            )
            send(line, line, p2s_sem.at[0], p2_sem.at[k], target)
            return carry

        lax.fori_loop(1, 4, step, 0)

    across(0, 0)
    lax.fori_loop(1, Z, z_start, 0)

    def z_wait(k):
        wait(xg.at[0, 0, 0], z_sem.at[k])

    z_wait(1)
    across(1, 1)

    def forward(i, carry):
        k = 2 * i
        z_wait(k)
        across(k, 0)
        along(k - 2, 0)
        z_wait(k + 1)
        across(k + 1, 1)
        along(k - 1, 1)
        return carry

    same = lax.rem(z + c, 2)
    first_own, second_own = same, 3 - same
    first_sib, second_sib = 1 - same, 2 + same

    def head(g, carry):
        chunks = []
        for i in range(4):
            k = 4 * g + i
            wait(xg.at[pl.ds(0, 3), :, 0], p2_sem.at[k])
        for i in range(4):
            zs = zmate(offset(4 * g + i))
            chunks.append(
                jnp.concatenate(
                    [xg[dx, dy, zs] for dx in range(X) for dy in range(Y)], axis=1
                )
            )
        lhs = jnp.concatenate(chunks, axis=0)
        for cc in range(2):
            out = dot(lhs, wbuf[cc])
            for i in range(4):
                zs = zmate(offset(4 * g + i))
                lp[zs, :, cc * COLS : (cc + 1) * COLS] = out[48 * i : 48 * i + 48]
        for pos in (first_sib, second_sib):
            zs = zmate(offset(4 * g + pos))
            send(
                lp.at[zs],
                lr.at[lax.div(zs, 2)],
                ls_sem.at[0],
                l_sem.at[g],
                dev(x, y, z, sib),
            )
        return carry

    def stats(g, carry):
        wait(lr.at[pl.ds(0, 2)], l_sem.at[g])
        lane = iota((48, 128), 1)
        for pos in (first_own, second_own):
            zs = zmate(offset(4 * g + pos))
            zi = lax.div(zs, 2)
            full = lp[zs] + lr[zi]
            top = jnp.max(full, axis=1, keepdims=True)
            shifted = full - top
            weights = jnp.exp(shifted)
            total = jnp.sum(weights, axis=1, keepdims=True)
            spread = jnp.sum(weights * shifted, axis=1, keepdims=True)
            packed = jnp.where(lane == 0, top, jnp.where(lane == 1, total, spread))
            for r in range(ROUNDS):
                lf[r, zi] = full[16 * r : 16 * r + 16]
                quant[r, zi] = packed[16 * r : 16 * r + 16]
        return carry

    own_w.wait()
    swap_w.wait_recv()
    lax.fori_loop(1, 8, forward, 0)
    along(14, 0)
    along(15, 1)
    lax.fori_loop(0, 4, head, 0)
    lax.fori_loop(0, 4, stats, 0)

    def held(index, core):
        return (lax.div(index, 16) * 2 + core) * 16 + lax.rem(index, 16)

    own_parent = (held(iota((128, 256), 0), c) == parent_row).astype(F32)
    column = iota((512, 256), 0)
    column = (
        ((y * 2 + lax.div(column, COLS)) * (X * Z) + v) * COLS + lax.rem(column, COLS)
    )
    st_send[...] = jnp.zeros((16, 128), F32)
    for r in range(ROUNDS):
        turned = quant[r].reshape(128, 128).T
        for i in range(3):
            st_send[3 * i + r : 3 * i + r + 1] = turned[i : i + 1]
        by_column = lf[r].reshape(128, 512).T
        picks = dot(by_column, own_parent, HIGHEST)
        picks = jnp.where(column == draft[r : r + 1], picks, 0.0)
        picks = jnp.sum(picks, axis=0, keepdims=True)
        st_send[9 + 2 * r : 10 + 2 * r] = picks[:, 0:128]
        st_send[10 + 2 * r : 11 + 2 * r] = picks[:, 128:256]

    def merge(ref):
        tile = ref[...]
        tops = tile[:, 0:3]
        top = jnp.max(tops, axis=0)
        shift = tops - top[None]
        factor = jnp.exp(shift)
        totals = tile[:, 3:6]
        total = jnp.sum(totals * factor, axis=0)
        spread = jnp.sum(factor * (tile[:, 6:9] + shift * totals), axis=0)
        picks = jnp.sum(tile[:, 9:16], axis=0)
        return jnp.concatenate([top, total, spread, picks], axis=0)

    mine = x * Y + y

    def sp_start(i, carry):
        j = lax.rem(mine + i, 16)
        send(
            st_send,
            st_plane.at[mine],
            sp_sem.at[0],
            sp_sem.at[1],
            dev(lax.div(j, Y), lax.rem(j, Y), z, c),
        )
        return carry

    lax.fori_loop(1, 16, sp_start, 0)
    st_plane[mine] = st_send[...]
    wait(st_plane.at[pl.ds(0, 15)], sp_sem.at[1])
    st_mid[...] = merge(st_plane)

    def sz_start(i, carry):
        send(
            st_mid, st_z.at[z], sz_sem.at[0], sz_sem.at[1], dev(x, y, zmate(i), c)
        )
        return carry

    lax.fori_loop(1, Z, sz_start, 0)
    st_z[z] = st_mid[...]
    wait(st_z.at[pl.ds(0, 15)], sz_sem.at[1])
    final = merge(st_z)
    st_own[...] = final
    send(st_own, st_sib, sb_sem.at[0], sb_sem.at[1], dev(x, y, z, sib))

    columns = jnp.concatenate([final, jnp.zeros((112, 128), F32)], axis=0).T
    other = pl.ds(pl.multiple_of(sib * COLS, COLS), COLS)
    ours = pl.ds(pl.multiple_of(c * COLS, COLS), COLS)
    for r in range(ROUNDS):
        top = columns[:, r : r + 1]
        inverse = 1.0 / columns[:, 3 + r : 4 + r]
        part = lf[r, :, :, other].reshape(128, COLS)
        psend[r] = (jnp.exp(part - top) * inverse).astype(BF16).reshape(8, 16, COLS)
    send(
        psend, prob.at[:, :, c], pr_sem.at[0], pr_sem.at[1], dev(x, y, z, sib)
    )
    for r in range(ROUNDS):
        top = columns[:, r : r + 1]
        inverse = 1.0 / columns[:, 3 + r : 4 + r]
        part = lf[r, :, :, ours].reshape(128, COLS)
        prob[r, :, c] = (jnp.exp(part - top) * inverse).astype(BF16).reshape(8, 16, COLS)

    wait(st_sib, sb_sem.at[1])
    even = jnp.where(c == 0, st_own[...], st_sib[...])
    odd = jnp.where(c == 0, st_sib[...], st_own[...])
    both = jnp.concatenate([even, odd], axis=1)
    log_total = jnp.log(both[3:6])
    log_norm = both[0:3] + log_total
    entropy = log_total - both[6:9] / both[3:6]
    stack = jnp.concatenate(
        [entropy, log_norm, jnp.zeros((2, 256), F32)], axis=0
    )
    place = iota((256, 256), 0)
    place = held(lax.rem(place, 128), lax.div(place, 128))
    in_order = dot(stack, (place == iota((256, 256), 1)).astype(F32), HIGHEST)
    of_parent = dot(stack, (place == parent_row).astype(F32), HIGHEST)
    picked = jnp.concatenate([even[9:15], odd[9:15]], axis=0)
    picked = jnp.concatenate(
        [
            jnp.concatenate(
                [
                    even[9 + 2 * r : 10 + 2 * r] + odd[9 + 2 * r : 10 + 2 * r],
                    even[10 + 2 * r : 11 + 2 * r] + odd[10 + 2 * r : 11 + 2 * r],
                ],
                axis=1,
            )
            for r in range(ROUNDS)
        ],
        axis=0,
    )
    log_draft = picked - of_parent[3:6]
    entropy_out[...] = in_order[0:3]
    margin_out[...] = log_draft + of_parent[0:3] - math.log(typical_alpha)

    tree = lax.div(iota((1, 256), 1), NODES)
    limits = []
    for r in range(ROUNDS):
        limit = jnp.zeros((1, 256), jnp.int32)
        for b in range(4):
            limit = jnp.where(tree == b, accepted[r, b], limit)
        limits.append(limit)
    limit = jnp.concatenate(limits, axis=0).astype(F32)
    survive = depth[0:3] < limit
    chosen = jnp.where(survive, log_draft, 0.0)
    in_tree = (lax.div(iota((256, 128), 0), NODES) == iota((256, 128), 1)).astype(F32)
    counted = dot(survive.astype(F32), in_tree, HIGHEST)
    score = dot(chosen, in_tree, HIGHEST)
    score_out[...] = score[:, 0:4] / counted[:, 0:4]

    wait(prob.at[:, :, 0], pr_sem.at[1])
    wait(psend, pr_sem.at[0])
    wait(st_own, sb_sem.at[0])
    wait(st_z.at[pl.ds(0, 15)], sz_sem.at[0])
    wait(st_plane.at[pl.ds(0, 15)], sp_sem.at[0])
    wait(lr, ls_sem.at[0])
    wait(xg.at[pl.ds(0, 3)], p2s_sem.at[0])
    wait(xg.at[0, pl.ds(0, 3)], p1s_sem.at[0])
    wait(xg.at[0, 0, pl.ds(0, 15)], zs_sem.at[0])
    wait(ss_recv.at[pl.ds(0, PLANE - 1)], ss_sem.at[0])
    wait(rs_recv.at[pl.ds(0, PLANE - 1)], rs_sem.at[0])
    swap_w.wait_send()


def body(partials, norm_gain, head_weight, draft_ids, tree_parents, accepted_lengths):
    vmem = pl.BlockSpec(memory_space=pltpu.VMEM)
    prob, entropy, margin, score = pl.pallas_call(
        kernel,
        out_shape=(
            jax.ShapeDtypeStruct((ROUNDS, 8, 2, 16, COLS), BF16),
            jax.ShapeDtypeStruct((ROUNDS, 256), F32),
            jax.ShapeDtypeStruct((ROUNDS, 256), F32),
            jax.ShapeDtypeStruct((ROUNDS, 4), F32),
        ),
        in_specs=[
            vmem,
            vmem,
            pl.BlockSpec(memory_space=pl.ANY),
            vmem,
            vmem,
            pl.BlockSpec(memory_space=pltpu.SMEM),
        ],
        out_specs=(vmem, vmem, vmem, vmem),
        scratch_shapes=[
            pltpu.VMEM((2, KHALF, COLS), BF16),
            pltpu.VMEM((PLANE, 16, 128), BF16),
            pltpu.VMEM((PLANE, 16, 128), BF16),
            pltpu.VMEM((8, 128), F32),
            pltpu.VMEM((PLANE, 8, 128), F32),
            pltpu.VMEM((X, Y, Z, 48, 128), BF16),
            pltpu.VMEM((Z, 48, 512), F32),
            pltpu.VMEM((8, 48, 512), F32),
            pltpu.VMEM((ROUNDS, 8, 16, 512), F32),
            pltpu.VMEM((ROUNDS, 8, 16, 128), F32),
            pltpu.VMEM((16, 128), F32),
            pltpu.VMEM((16, 16, 128), F32),
            pltpu.VMEM((16, 128), F32),
            pltpu.VMEM((Z, 16, 128), F32),
            pltpu.VMEM((16, 128), F32),
            pltpu.VMEM((16, 128), F32),
            pltpu.VMEM((ROUNDS, 8, 16, COLS), BF16),
            pltpu.SemaphoreType.DMA((3,)),
            pltpu.SemaphoreType.DMA((2,)),
            pltpu.SemaphoreType.DMA((2,)),
            pltpu.SemaphoreType.DMA((Z,)),
            pltpu.SemaphoreType.DMA((1,)),
            pltpu.SemaphoreType.DMA((Z,)),
            pltpu.SemaphoreType.DMA((1,)),
            pltpu.SemaphoreType.DMA((Z,)),
            pltpu.SemaphoreType.DMA((1,)),
            pltpu.SemaphoreType.DMA((4,)),
            pltpu.SemaphoreType.DMA((1,)),
            pltpu.SemaphoreType.DMA((2,)),
            pltpu.SemaphoreType.DMA((2,)),
            pltpu.SemaphoreType.DMA((2,)),
            pltpu.SemaphoreType.DMA((2,)),
        ],
        compiler_params=pltpu.CompilerParams(
            collective_id=0, has_side_effects=True, vmem_limit_bytes=40 * 2**20
        ),
        name="verify",
    )(
        partials,
        norm_gain.astype(F32).reshape(PLANE, 1, 128),
        head_weight,
        draft_ids,
        tree_parents.reshape(1, 256),
        accepted_lengths,
    )
    return prob.reshape(ROUNDS, 256, COLS), entropy, margin, score


def solution(mesh):
    placed = (P(None, "tensor", "vocab", None), P(), P(None, ("tensor", "vocab")), P(), P(), P())
    return jax.shard_map(
        body,
        mesh=mesh,
        in_specs=placed,
        out_specs=(P(None, None, ("tensor", "vocab")), P(), P(), P()),
        check_vma=False,
    )
```

time: 761 us -> 95.6 us (0.13)
  waiting for transfers between devices: 445 us -> 0 us
  blocking collectives: 209 us -> 0 us
  Pallas kernels: 0 us -> 87 us
  local copies, waits for them, and re-layouts: 75.1 us -> 7.04 us
  between operations: 14.3 us -> 0.65 us
  matrix products: 8.45 us -> 0 us
  other arithmetic: 8.51 us -> 0.7 us
    all_gather x3 -> x0, waiting for transfers between devices: 364 us -> none  [body(): lax.all_gather(full_rows, 'vocab', axis=0, tiled=True)]
    pmax x1 -> x0, blocking collectives: 110 us -> none  [body(): row_max = lax.pmax(local_max, ('tensor', 'vocab'))]
    psum x1 -> x0, blocking collectives: 99 us -> none  [body(): lax.psum((local_total * rescale, rescale * (local_spread + (local_max - r...]
    pallas_call x0 -> x1, Pallas kernels: none -> 87 us  [body(): pl.pallas_call(kernel, out_shape=(jax.ShapeDtypeStruct((ROUNDS, 8, 2, 16,...]
    psum x1 -> x0, waiting for transfers between devices: 80.7 us -> none  [body(): hidden = lax.psum(piece, 'tensor')]
    gather x45 -> x0, local copies, waits for them, and re-layouts: 55.9 us -> none  [the longest x21 18.2 us: tree_depth(): depth = depth + jnp.take_along_axis(depth, parents, axis=1)]
    unnamed x22 -> x14, local copies, waits for them, and re-layouts: 17.1 us -> 7.04 us
    dot_general x6 -> x0, matrix products: 8.45 us -> none  [the longest x3 7.59 us: body(): jnp.dot(lax.all_gather(full_rows, 'vocab', axis=0, tiled=True), head_weig...]
  transfers between devices with their start and end apart: 4 -> 0, of which waited for: 4 -> 0; matrix products, arithmetic and copies ran while one was open for 6% -> 0% of each run, Pallas kernels for 0% -> 0%
where the time goes in v1:
time: 95.6 us; the launch traced here: 95.3 us
  Pallas kernels  87 us (91%)
  local copies, waits for them, and re-layouts  7.04 us (7%)
    pallas_call x1, Pallas kernels, body(): pl.pallas_call(kernel, out_shape=(jax.ShapeDtypeStruct((ROUNDS, 8, 2, 16,...  87 us
    unnamed x14, local copies, waits for them, and re-layouts  7.04 us

profile of v1, /device:TPU:1, one launch (start us, length us, event | category | flops | bytes accessed | tf_op | source)
XLA Modules:
  0.0 95.3 jit_solution(510802246842661432)
XLA Ops:
  0.6 0.7 reshape.23
  1.3 0.0 copy-start
  1.3 1.6 %copy-done = bf16[4096,256]{1,0:T(8,128)(2,1)S(1)} copy-done((bf16[4096,256]{1,0:T(8,128)(2,1)S(1)}, bf16[4096,256]{1,0:T(8,128)(2,1)}, u32[]{:S(2)}) %copy-start) | copy-done | bytes 2097176
  2.9 0.0 copy-start.1
  2.9 0.9 copy-done.1
  3.8 0.0 copy-start.2
  3.8 0.7 copy-done.2
  4.5 0.0 copy-start.3
  4.5 0.7 copy-done.3
  5.2 0.0 copy-start.4
  5.2 0.7 copy-done.4
  5.9 87.0 %verify.1 = (bf16[3,8,2,16,256]{4,3,2,1,0:T(8,128)(2,1)S(1)}, f32[3,256]{1,0:T(4,128)S(1)}, f32[3,256]{1,0:T(4,128)S(1)}, f32[3,4]{1,0:T(4,128)S(1)}) custom-call(bf16[3,1,4,4096]{3,2,1,0:T(4,128)(2,1)S(1)} %copy-done.1, f32[32,1,128]{2,1,0:T(1,128)S(1)} %bitcast.4, bf16[4096,256]{1,0:T(8,128)(2,1)S(1)} %copy-done, s32[3,256]{1,0:T(4,128)S(1)} %copy-done.2, ...), custom_call_target="tpu_custom_call" | custom-call | tf_op jit(solution)/shard_map/verify/pallas_call | solution.py:476
  92.8 0.7 copy.14
  93.6 0.6 copy.15
  94.2 0.6 copy.16
  94.8 0.6 copy.17
Async XLA Ops:
  1.3 1.6 %copy-start = (bf16[4096,256]{1,0:T(8,128)(2,1)S(1)}, bf16[4096,256]{1,0:T(8,128)(2,1)}, u32[]{:S(2)}) copy-start(bf16[4096,256]{1,0:T(8,128)(2,1)} %weight.1) | copy-start | bytes 6291460
  2.9 0.9 copy-start.1
  3.8 0.7 copy-start.2
  4.5 0.7 copy-start.3
  5.2 0.7 copy-start.4

commit v2 on v1

v2 whole, which is shorter than its diff:
```python
import math

import jax
import jax.numpy as jnp
from jax import lax
from jax.experimental import pallas as pl
from jax.experimental.pallas import tpu as pltpu
from jax.sharding import PartitionSpec as P

MESH = pl.DeviceIdType.MESH
HIGHEST = lax.Precision.HIGHEST
F32 = jnp.float32
BF16 = jnp.bfloat16

X = 4
Y = 4
Z = 16
PLANE = 32
KHALF = 2048
COLS = 256
ROUNDS = 3
NODES = 64
SEQ = (0, 1, -1, 5, -5, 3, -3, 4, -4, 7, -7, 8)
GIFTS = {1: (-1, 0), -1: (1, 1), 5: (-1, 2), -5: (1, 3)}
GIVEN = {2: 0, -2: 1, 6: 2, -6: 3}
GROUPS = ((0, 1, -1, 4), (2, 5, -5, -2), (-4, 3, -3, 8), (6, 7, -7, -6))
position = {o: n for n, o in enumerate(SEQ)}
position.update({2: 1, -2: 2, 6: 3, -6: 4})
LAG = 3
DONE = 2
HEADS = ((3, 0, 1), (5, 1, 2), (99, 2, 3), (99, 3, 4))
norm_eps = 1e-06
typical_alpha = 0.3


def dot(a, b, precision=None):
    return jnp.dot(a, b, precision=precision, preferred_element_type=F32)


def iota(shape, dim):
    return lax.broadcasted_iota(jnp.int32, shape, dim)


def kernel(
    partials,
    gain,
    weight,
    draft_in,
    parents_in,
    accepted_in,
    prob,
    small,
    pbuf,
    gbuf,
    draft,
    parents,
    accepted,
    wbuf,
    rs_send,
    rs_recv,
    ss_send,
    ss_recv,
    xg,
    lp,
    lr,
    lf,
    quant,
    st_send,
    st_plane,
    st_mid,
    st_z,
    st_own,
    st_sib,
    pk_send,
    pk_plane,
    pk_mid,
    pk_z,
    pk_own,
    pk_sib,
    psend,
    in_sem,
    w_sem,
    rs_sem,
    ss_sem,
    z_sem,
    zs_sem,
    p1_sem,
    p1s_sem,
    p2_sem,
    p2s_sem,
    p3_sem,
    p3s_sem,
    g_sem,
    gs_sem,
    l_sem,
    ls_sem,
    sp_sem,
    sz_sem,
    sb_sem,
    kp_sem,
    kz_sem,
    kb_sem,
    pr_sem,
):
    t = lax.axis_index("tensor")
    v = lax.axis_index("vocab")
    x = lax.rem(v, X)
    z = lax.div(v, X)
    y = lax.div(t, 2)
    c = lax.rem(t, 2)
    sib = 1 - c

    def dev(dx, dy, dz, dc):
        return (dy * 2 + dc, dz * X + dx)

    def wait(ref, sem):
        pltpu.make_async_copy(ref, ref, sem).wait()

    def send(src, dst, ssem, rsem, device):
        pltpu.make_async_remote_copy(
            src_ref=src,
            dst_ref=dst,
            send_sem=ssem,
            recv_sem=rsem,
            device_id=device,
            device_id_type=MESH,
        ).start()

    me = c * 16 + x * Y + y

    def plane_dev(j):
        return dev(lax.div(lax.rem(j, 16), Y), lax.rem(j, Y), z, lax.div(j, 16))

    def zmate(o):
        return lax.rem(z + o + Z, Z)

    barrier = pltpu.get_barrier_semaphore()

    def greet_plane(i, carry):
        j = lax.rem(me + i, PLANE)
        pl.semaphore_signal(barrier, inc=1, device_id=plane_dev(j), device_id_type=MESH)
        return carry

    def greet_z(i, carry):
        pl.semaphore_signal(
            barrier, inc=1, device_id=dev(x, y, zmate(i), c), device_id_type=MESH
        )
        return carry

    read_partials = pltpu.make_async_copy(partials.at[:, 0], pbuf, in_sem.at[0])
    read_partials.start()
    lax.fori_loop(1, Z, greet_z, 0)
    lax.fori_loop(1, PLANE, greet_plane, 0)
    reads = [
        pltpu.make_async_copy(src, dst, in_sem.at[1 + i])
        for i, (src, dst) in enumerate(
            ((gain, gbuf), (draft_in, draft), (parents_in, parents), (accepted_in, accepted))
        )
    ]
    for read in reads:
        read.start()

    own_w = pltpu.make_async_copy(
        weight.at[pl.ds(c * KHALF, KHALF)], wbuf.at[c], w_sem.at[0]
    )
    own_w.start()

    read_partials.wait()
    rows = [pbuf[r].astype(F32) for r in range(ROUNDS)]
    slab = jnp.concatenate(rows + [jnp.zeros_like(rows[0])], axis=0).astype(BF16)
    for j in range(PLANE):
        rs_send[j] = slab[:, j * 128 : (j + 1) * 128]

    common = iota((128, 128), 0) & iota((128, 128), 1)
    parity = jnp.zeros((128, 128), jnp.int32)
    for bit in range(7):
        parity = parity + (lax.shift_right_logical(common, bit) & 1)
    signs = (1 - 2 * (parity & 1)).astype(F32)

    for read in reads:
        read.wait()
    gains = gbuf[...].astype(F32).reshape(PLANE, 128)
    gain_row = jnp.sum(
        jnp.where(iota((PLANE, 128), 0) == me, gains, 0.0), axis=0, keepdims=True
    )

    pl.semaphore_wait(barrier, PLANE - 1 + Z - 1)

    def rs_start(i, carry):
        j = lax.rem(me + i, PLANE)
        send(rs_send.at[j], rs_recv.at[me], rs_sem.at[0], rs_sem.at[1], plane_dev(j))
        return carry

    lax.fori_loop(1, PLANE, rs_start, 0)
    rs_recv[me] = rs_send[me]

    swap_w = pltpu.make_async_remote_copy(
        src_ref=weight.at[pl.ds(sib * KHALF, KHALF)],
        dst_ref=wbuf.at[c],
        send_sem=w_sem.at[1],
        recv_sem=w_sem.at[2],
        device_id=dev(x, y, z, sib),
        device_id_type=MESH,
    )
    wait(rs_recv.at[pl.ds(0, PLANE - 1)], rs_sem.at[1])
    swap_w.start()

    pieces = []
    for dx in range(X):
        total = jnp.zeros((16, 128), F32)
        for dy in range(Y):
            for dc in range(2):
                total = total + rs_recv[dc * 16 + dx * Y + dy].astype(F32)
        pieces.append(total)
    hidden = jnp.concatenate(
        [pieces[dx][4 * r : 4 * r + 4] for r in range(ROUNDS) for dx in range(X)],
        axis=0,
    )
    square = jnp.concatenate([hidden * hidden, jnp.zeros((80, 128), F32)], axis=0)
    ss_send[...] = jnp.broadcast_to(
        jnp.sum(square.T, axis=0, keepdims=True), (8, 128)
    )

    def ss_start(i, carry):
        j = lax.rem(me + i, PLANE)
        send(ss_send, ss_recv.at[me], ss_sem.at[0], ss_sem.at[1], plane_dev(j))
        return carry

    lax.fori_loop(1, PLANE, ss_start, 0)
    ss_recv[me] = ss_send[...]
    wait(ss_recv.at[pl.ds(0, PLANE - 1)], ss_sem.at[1])
    sums = ss_recv[0]
    for j in range(1, PLANE):
        sums = sums + ss_recv[j]
    scale = lax.rsqrt(sums[0:1] * (1.0 / 4096.0) + norm_eps)
    scale = jnp.broadcast_to(scale, (128, 128)).T[0:48]
    normed = hidden * scale * gain_row
    rotated = dot(normed, signs, HIGHEST) * (1.0 / math.sqrt(128.0))
    def order_of(n):
        return lax.rem(n + c, 2)

    def place(o, dx, dy):
        order = order_of(position[o])
        return dy + order * (dx - dy), dx + order * (dy - dx)

    def plane_step(axis_is_y, i):
        return dev(
            lax.rem(x + i * (1 - axis_is_y), X), lax.rem(y + i * axis_is_y, Y), z, c
        )

    def chunk_at(o):
        line, spot = place(o, x, y)
        return xg.at[zmate(o), line, spot]

    mine = xg.at[z, place(0, x, y)[0], place(0, x, y)[1]]
    mine[...] = rotated.astype(BF16)

    def z_start(n):
        line, spot = place(SEQ[n], x, y)
        send(
            mine,
            xg.at[z, line, spot],
            zs_sem.at[0],
            z_sem.at[n],
            dev(x, y, zmate(-SEQ[n]), c),
        )

    def across(n):
        chunk = chunk_at(SEQ[n])

        def step(i, carry):
            send(chunk, chunk, p1s_sem.at[0], p1_sem.at[n], plane_step(order_of(n), i))
            return carry

        lax.fori_loop(1, 4, step, 0)

    def along(n):
        wait(xg.at[0, 0, pl.ds(0, 3)], p1_sem.at[n])
        line = xg.at[zmate(SEQ[n]), place(SEQ[n], x, y)[0]]
        for i in range(2):
            send(
                line,
                line,
                p2s_sem.at[0],
                p2_sem.at[n, i],
                plane_step(1 - order_of(n), 1 + 2 * i),
            )

    def onward(n):
        here = place(SEQ[n], x, y)[0]
        for i in range(2):
            wait(xg.at[0, 0], p2_sem.at[n, i])
            half = xg.at[zmate(SEQ[n]), lax.rem(here + 3 - 2 * i, 4), pl.ds(2 * i, 2)]
            send(
                half,
                half,
                p3s_sem.at[0],
                p3_sem.at[n],
                plane_step(1 - order_of(n), 1 + 2 * i),
            )

    def complete(n):
        wait(xg.at[0, 0], p3_sem.at[n])
        if SEQ[n] in GIFTS:
            step, index = GIFTS[SEQ[n]]
            whole = xg.at[zmate(SEQ[n])]
            send(whole, whole, gs_sem.at[0], g_sem.at[index], dev(x, y, zmate(step), c))

    same = lax.rem(z + c, 2)

    def own_plane(g, i):
        group = GROUPS[g]
        return zmate(group[3 * i] + same * (group[1 + i] - group[3 * i]))

    def sib_plane(g, i):
        group = GROUPS[g]
        return zmate(group[1 + i] + same * (group[3 * i] - group[1 + i]))

    def head(first, last):
        offsets = [o for g in range(first, last) for o in GROUPS[g]]
        for o in offsets:
            if o in GIVEN:
                wait(xg.at[0], g_sem.at[GIVEN[o]])
        chunks = []
        for o in offsets:
            pieces = []
            for dx in range(X):
                for dy in range(Y):
                    line, spot = place(o, dx, dy)
                    pieces.append(xg[zmate(o), line, spot])
            chunks.append(jnp.concatenate(pieces, axis=1))
        lhs = jnp.concatenate(chunks, axis=0)
        for cc in range(2):
            out = dot(lhs, wbuf[cc])
            for i, o in enumerate(offsets):
                lp[zmate(o), :, cc * COLS : (cc + 1) * COLS] = out[48 * i : 48 * i + 48]
        for g in range(first, last):
            for i in range(2):
                zs = sib_plane(g, i)
                send(
                    lp.at[zs],
                    lr.at[lax.div(zs, 2)],
                    ls_sem.at[0],
                    l_sem.at[g],
                    dev(x, y, z, sib),
                )

    def stats(g):
        wait(lr.at[pl.ds(0, 2)], l_sem.at[g])
        lane = iota((48, 128), 1)
        for i in range(2):
            zs = own_plane(g, i)
            zi = lax.div(zs, 2)
            full = lp[zs] + lr[zi]
            top = jnp.max(full, axis=1, keepdims=True)
            shifted = full - top
            weights = jnp.exp(shifted)
            total = jnp.sum(weights, axis=1, keepdims=True)
            spread = jnp.sum(weights * shifted, axis=1, keepdims=True)
            log_total = jnp.log(total)
            packed = jnp.where(lane == 0, top + log_total, log_total - spread / total)
            for r in range(ROUNDS):
                lf[r, zi] = full[16 * r : 16 * r + 16]
                quant[r, zi] = packed[16 * r : 16 * r + 16]

    count = len(SEQ)
    across(0)
    for n in range(1, count):
        z_start(n)
    for step in range(1, count + 2 * LAG + DONE):
        if step < count:
            wait(mine, z_sem.at[step])
            across(step)
        if LAG <= step < count + LAG:
            along(step - LAG)
        if 2 * LAG <= step < count + 2 * LAG:
            onward(step - 2 * LAG)
        if 2 * LAG + DONE <= step:
            complete(step - 2 * LAG - DONE)
        if step == count:
            own_w.wait()
            swap_w.wait_recv()
        for at, first, last in HEADS:
            if step == at + count:
                head(first, last)
    ready = 0
    for at, first, last in HEADS:
        if at + count >= count + 2 * LAG + DONE:
            head(first, last)
            for g in range(ready, last - 1):
                stats(g)
            ready = last - 1
    stats(len(GROUPS) - 1)

    chip = x * Y + y

    def plane_start(src, dst, sems):
        def step(i, carry):
            j = lax.rem(chip + i, 16)
            send(
                src,
                dst.at[chip],
                sems.at[0],
                sems.at[1],
                dev(lax.div(j, Y), lax.rem(j, Y), z, c),
            )
            return carry

        lax.fori_loop(1, 16, step, 0)
        dst[chip] = src[...]

    def line_start(src, dst, sems):
        def step(i, carry):
            send(src, dst.at[z], sems.at[0], sems.at[1], dev(x, y, zmate(i), c))
            return carry

        lax.fori_loop(1, Z, step, 0)
        dst[z] = src[...]

    def merge(ref):
        tile = ref[...]
        part_log, part_entropy = tile[:, 0:3], tile[:, 3:6]
        top = jnp.max(part_log, axis=0)
        share = jnp.exp(part_log - top[None])
        total = jnp.sum(share, axis=0)
        log_norm = top + jnp.log(total)
        spread = jnp.sum(share * (part_entropy + (log_norm[None] - part_log)), axis=0)
        return jnp.concatenate(
            [log_norm, spread / total, jnp.zeros((2, 128), F32)], axis=0
        )

    st_send[...] = jnp.zeros((8, 128), F32)
    for r in range(ROUNDS):
        turned = quant[r].reshape(128, 128).T
        for i in range(2):
            st_send[3 * i + r : 3 * i + r + 1] = turned[i : i + 1]
    plane_start(st_send, st_plane, sp_sem)

    def held(index, core):
        return (lax.div(index, 16) * 2 + core) * 16 + lax.rem(index, 16)

    parent_row = lax.div(iota((1, 256), 1), NODES) * NODES + parents[...]
    own_parent = (held(iota((128, 256), 0), c) == parent_row).astype(F32)
    column = iota((512, 256), 0)
    column = (
        ((y * 2 + lax.div(column, COLS)) * (X * Z) + v) * COLS + lax.rem(column, COLS)
    )
    pk_send[...] = jnp.zeros((8, 128), F32)
    for r in range(ROUNDS):
        by_column = lf[r].reshape(128, 512).T
        picks = dot(by_column, own_parent, HIGHEST)
        picks = jnp.where(column == draft[r : r + 1], picks, 0.0)
        picks = jnp.sum(picks, axis=0, keepdims=True)
        pk_send[2 * r : 2 * r + 1] = picks[:, 0:128]
        pk_send[2 * r + 1 : 2 * r + 2] = picks[:, 128:256]
    plane_start(pk_send, pk_plane, kp_sem)

    wait(st_plane.at[pl.ds(0, 15)], sp_sem.at[1])
    st_mid[...] = merge(st_plane)
    line_start(st_mid, st_z, sz_sem)
    wait(pk_plane.at[pl.ds(0, 15)], kp_sem.at[1])
    pk_mid[...] = jnp.sum(pk_plane[...], axis=0)
    line_start(pk_mid, pk_z, kz_sem)

    jump = (iota((256, 256), 0) == parent_row).astype(BF16)
    depth = jnp.broadcast_to(
        (lax.rem(iota((1, 256), 1), NODES) > 0).astype(F32), (8, 256)
    )
    for step in range(NODES.bit_length()):
        depth = depth + dot(depth.astype(BF16), jump)
        if step < NODES.bit_length() - 1:
            jump = dot(jump, jump).astype(BF16)

    wait(st_z.at[pl.ds(0, 15)], sz_sem.at[1])
    final = merge(st_z)
    st_own[...] = final
    send(st_own, st_sib, sb_sem.at[0], sb_sem.at[1], dev(x, y, z, sib))

    columns = jnp.concatenate([final, jnp.zeros((120, 128), F32)], axis=0).T
    other = pl.ds(pl.multiple_of(sib * COLS, COLS), COLS)
    ours = pl.ds(pl.multiple_of(c * COLS, COLS), COLS)
    for r in range(ROUNDS):
        part = lf[r, :, :, other].reshape(128, COLS) - columns[:, r : r + 1]
        psend[r] = jnp.exp(part).astype(BF16).reshape(8, 16, COLS)
    send(
        psend, prob.at[:, :, c], pr_sem.at[0], pr_sem.at[1], dev(x, y, z, sib)
    )
    for r in range(ROUNDS):
        part = lf[r, :, :, ours].reshape(128, COLS) - columns[:, r : r + 1]
        prob[r, :, c] = jnp.exp(part).astype(BF16).reshape(8, 16, COLS)

    wait(pk_z.at[pl.ds(0, 15)], kz_sem.at[1])
    pk_own[...] = jnp.sum(pk_z[...], axis=0)
    send(pk_own, pk_sib, kb_sem.at[0], kb_sem.at[1], dev(x, y, z, sib))

    wait(st_sib, sb_sem.at[1])
    even = jnp.where(c == 0, st_own[...], st_sib[...])
    odd = jnp.where(c == 0, st_sib[...], st_own[...])
    both = jnp.concatenate([even, odd], axis=1)
    spots = iota((256, 256), 0)
    spots = held(lax.rem(spots, 128), lax.div(spots, 128))
    in_order = dot(both, (spots == iota((256, 256), 1)).astype(F32), HIGHEST)
    of_parent = dot(both, (spots == parent_row).astype(F32), HIGHEST)

    tree = lax.div(iota((1, 256), 1), NODES)
    limits = []
    for r in range(ROUNDS):
        limit = jnp.zeros((1, 256), jnp.int32)
        for b in range(4):
            limit = jnp.where(tree == b, accepted[r : r + 1, b : b + 1], limit)
        limits.append(limit)
    limit = jnp.concatenate(limits, axis=0).astype(F32)
    survive = depth[0:3] < limit
    lane = iota((256, 128), 1)
    in_tree = (lax.div(iota((256, 128), 0), NODES) == lax.rem(lane, 4)).astype(F32)
    counted = dot(survive.astype(F32), in_tree, HIGHEST)

    wait(pk_sib, kb_sem.at[1])
    picks = jnp.where(c == 0, pk_own[...], pk_sib[...])
    picks = picks + jnp.where(c == 0, pk_sib[...], pk_own[...])
    picked = jnp.concatenate(
        [
            jnp.concatenate([picks[2 * r : 2 * r + 1], picks[2 * r + 1 : 2 * r + 2]], axis=1)
            for r in range(ROUNDS)
        ],
        axis=0,
    )
    log_draft = picked - of_parent[0:3]
    chosen = jnp.where(survive, log_draft, 0.0)
    score = dot(chosen, in_tree, HIGHEST) / counted
    small[0:3] = in_order[3:6]
    small[3:6] = log_draft + of_parent[3:6] - math.log(typical_alpha)
    small[8:11] = jnp.concatenate([score, score], axis=1)

    wait(prob.at[:, :, 0], pr_sem.at[1])
    wait(psend, pr_sem.at[0])
    wait(pk_own, kb_sem.at[0])
    wait(st_own, sb_sem.at[0])
    wait(pk_z.at[pl.ds(0, 15)], kz_sem.at[0])
    wait(st_z.at[pl.ds(0, 15)], sz_sem.at[0])
    wait(pk_plane.at[pl.ds(0, 15)], kp_sem.at[0])
    wait(st_plane.at[pl.ds(0, 15)], sp_sem.at[0])
    wait(lr, ls_sem.at[0])
    if GIFTS:
        wait(xg.at[pl.ds(0, len(GIFTS))], gs_sem.at[0])
    wait(xg.at[pl.ds(0, count), 0], p3s_sem.at[0])
    wait(xg.at[pl.ds(0, count), pl.ds(0, 2)], p2s_sem.at[0])
    wait(xg.at[pl.ds(0, count), 0, pl.ds(0, 3)], p1s_sem.at[0])
    wait(xg.at[pl.ds(0, count - 1), 0, 0], zs_sem.at[0])
    wait(ss_recv.at[pl.ds(0, PLANE - 1)], ss_sem.at[0])
    wait(rs_recv.at[pl.ds(0, PLANE - 1)], rs_sem.at[0])
    swap_w.wait_send()


def body(partials, norm_gain, head_weight, draft_ids, tree_parents, accepted_lengths):
    vmem = pl.BlockSpec(memory_space=pltpu.VMEM)
    hbm = pl.BlockSpec(memory_space=pltpu.HBM)
    tile = pltpu.VMEM((8, 128), F32)
    tiles = pltpu.VMEM((16, 8, 128), F32)
    one, two = pltpu.SemaphoreType.DMA((1,)), pltpu.SemaphoreType.DMA((2,))
    prob, small = pl.pallas_call(
        kernel,
        out_shape=(
            jax.ShapeDtypeStruct((ROUNDS, 8, 2, 16, COLS), BF16),
            jax.ShapeDtypeStruct((16, 256), F32),
        ),
        in_specs=[hbm] * 6,
        out_specs=(vmem, vmem),
        scratch_shapes=[
            pltpu.VMEM((ROUNDS, 4, 4096), BF16),
            pltpu.VMEM((4096,), BF16),
            pltpu.VMEM((ROUNDS, 256), jnp.int32),
            pltpu.VMEM((1, 256), jnp.int32),
            pltpu.VMEM((ROUNDS, 4), jnp.int32),
            pltpu.VMEM((2, KHALF, COLS), BF16),
            pltpu.VMEM((PLANE, 16, 128), BF16),
            pltpu.VMEM((PLANE, 16, 128), BF16),
            tile,
            pltpu.VMEM((PLANE, 8, 128), F32),
            pltpu.VMEM((Z, 4, 4, 48, 128), BF16),
            pltpu.VMEM((Z, 48, 512), F32),
            pltpu.VMEM((8, 48, 512), F32),
            pltpu.VMEM((ROUNDS, 8, 16, 512), F32),
            pltpu.VMEM((ROUNDS, 8, 16, 128), F32),
            tile,
            tiles,
            tile,
            tiles,
            tile,
            tile,
            tile,
            tiles,
            tile,
            tiles,
            tile,
            tile,
            pltpu.VMEM((ROUNDS, 8, 16, COLS), BF16),
            pltpu.SemaphoreType.DMA((5,)),
            pltpu.SemaphoreType.DMA((3,)),
            two,
            two,
            pltpu.SemaphoreType.DMA((Z,)),
            one,
            pltpu.SemaphoreType.DMA((Z,)),
            one,
            pltpu.SemaphoreType.DMA((Z, 2)),
            one,
            pltpu.SemaphoreType.DMA((Z,)),
            one,
            pltpu.SemaphoreType.DMA((4,)),
            one,
            pltpu.SemaphoreType.DMA((4,)),
            one,
            two,
            two,
            two,
            two,
            two,
            two,
            two,
        ],
        compiler_params=pltpu.CompilerParams(
            collective_id=0, has_side_effects=True, vmem_limit_bytes=40 * 2**20
        ),
        name="verify",
    )(
        *(
            pltpu.with_memory_space_constraint(a, pltpu.HBM)
            for a in (
                partials,
                norm_gain,
                head_weight,
                draft_ids,
                tree_parents.reshape(1, 256),
                accepted_lengths,
            )
        )
    )
    return (
        prob.reshape(ROUNDS, 256, COLS),
        small[0:3],
        small[3:6],
        small[8:11, 0:4],
    )


def solution(mesh):
    placed = (P(None, "tensor", "vocab", None), P(), P(None, ("tensor", "vocab")), P(), P(), P())
    return jax.shard_map(
        body,
        mesh=mesh,
        in_specs=placed,
        out_specs=(P(None, None, ("tensor", "vocab")), P(), P(), P()),
        check_vma=False,
    )
```

time: 95.6 us -> 78.8 us (0.82)
  Pallas kernels: 87 us -> 76.1 us
  local copies, waits for them, and re-layouts: 7.04 us -> 1.93 us
    pallas_call x1, Pallas kernels: 87 us -> 76.1 us  [body(): pl.pallas_call(kernel, out_shape=(jax.ShapeDtypeStruct((ROUNDS, 8, 2, 16,...]
    unnamed x14 -> x1, local copies, waits for them, and re-layouts: 7.04 us -> 0.75 us
    slice x0 -> x2, local copies, waits for them, and re-layouts: none -> 1.18 us  [the longest x1 0.6 us: body(): small[3:6]]
where the time goes in v2:
time: 78.8 us; the launch traced here: 78.7 us
  Pallas kernels  76.1 us (97%)
  local copies, waits for them, and re-layouts  1.93 us (2%)
    pallas_call x1, Pallas kernels, body(): pl.pallas_call(kernel, out_shape=(jax.ShapeDtypeStruct((ROUNDS, 8, 2, 16,...  76.1 us

profile of v2, /device:TPU:1, one launch (start us, length us, event | category | flops | bytes accessed | tf_op | source)
XLA Modules:
  0.0 78.7 jit_solution(18326214960254067242)
XLA Ops:
  0.6 76.1 %verify.1 = (bf16[3,8,2,16,256]{4,3,2,1,0:T(8,128)(2,1)S(1)}, f32[16,256]{1,0:T(8,128)S(1)}) custom-call(bf16[3,1,4,4096]{3,2,1,0:T(4,128)(2,1)} %partials.1, bf16[4096]{0:T(1024)(128)(2,1)} %gain.1, bf16[4096,256]{1,0:T(8,128)(2,1)} %weight.1, s32[3,256]{1,0:T(4,128)} %draft_in.1, s32[1,256]{1,0:T(1,128)} %bitcast.3, s32[3,4]{1,0:T(4,128)} %accepted_in.1), custom_call_target="tpu_custom_call" | custom-call | tf_op jit(solution)/shard_map/verify/pallas_call | solution.py:561
  76.8 0.6 fusion
  77.4 0.6 slice.11
  77.9 0.7 copy.11

commit v3 on v2

--- a/solution.py
+++ b/solution.py
@@ -20,14 +20,16 @@
 COLS = 256
 ROUNDS = 3
 NODES = 64
-SEQ = (0, 1, -1, 5, -5, 3, -3, 4, -4, 7, -7, 8)
+SEQ = (0, 1, -1, 3, -3, 5, -5, 4, -4, 7, -7, 8)
 GIFTS = {1: (-1, 0), -1: (1, 1), 5: (-1, 2), -5: (1, 3)}
 GIVEN = {2: 0, -2: 1, 6: 2, -6: 3}
-GROUPS = ((0, 1, -1, 4), (2, 5, -5, -2), (-4, 3, -3, 8), (6, 7, -7, -6))
+GROUPS = ((0, 1, -1, 4), (2, 3, -3, -2), (-4, 5, -5, 8), (6, 7, -7, -6))
 position = {o: n for n, o in enumerate(SEQ)}
-position.update({2: 1, -2: 2, 6: 3, -6: 4})
+position.update({2: 1, -2: 2, 6: 5, -6: 6})
 LAG = 3
 DONE = 2
+AHEAD = 11
+DIRECT = 0
 HEADS = ((3, 0, 1), (5, 1, 2), (99, 2, 3), (99, 3, 4))
 norm_eps = 1e-06
 typical_alpha = 0.3
@@ -75,8 +77,6 @@
     pk_plane,
     pk_mid,
     pk_z,
-    pk_own,
-    pk_sib,
     psend,
     in_sem,
     w_sem,
@@ -92,6 +92,7 @@
     p3s_sem,
     g_sem,
     gs_sem,
+    ds_sem,
     l_sem,
     ls_sem,
     sp_sem,
@@ -99,8 +100,8 @@
     sb_sem,
     kp_sem,
     kz_sem,
-    kb_sem,
     pr_sem,
+    near_sem,
 ):
     t = lax.axis_index("tensor")
     v = lax.axis_index("vocab")
@@ -141,15 +142,15 @@
         pl.semaphore_signal(barrier, inc=1, device_id=plane_dev(j), device_id_type=MESH)
         return carry
 
-    def greet_z(i, carry):
-        pl.semaphore_signal(
-            barrier, inc=1, device_id=dev(x, y, zmate(i), c), device_id_type=MESH
-        )
-        return carry
+    def greet_z(semaphore, distance):
+        for o in (distance, -distance):
+            pl.semaphore_signal(
+                semaphore, inc=1, device_id=dev(x, y, zmate(o), c), device_id_type=MESH
+            )
 
     read_partials = pltpu.make_async_copy(partials.at[:, 0], pbuf, in_sem.at[0])
     read_partials.start()
-    lax.fori_loop(1, Z, greet_z, 0)
+    greet_z(barrier, 1)
     lax.fori_loop(1, PLANE, greet_plane, 0)
     reads = [
         pltpu.make_async_copy(src, dst, in_sem.at[1 + i])
@@ -184,7 +185,8 @@
         jnp.where(iota((PLANE, 128), 0) == me, gains, 0.0), axis=0, keepdims=True
     )
 
-    pl.semaphore_wait(barrier, PLANE - 1 + Z - 1)
+    pl.semaphore_wait(barrier, PLANE - 1 + 2)
+    greet_z(near_sem.at[0], 1)
 
     def rs_start(i, carry):
         j = lax.rem(me + i, PLANE)
@@ -202,6 +204,8 @@
         device_id=dev(x, y, z, sib),
         device_id_type=MESH,
     )
+    pl.semaphore_wait(near_sem.at[0], 2)
+    greet_z(near_sem.at[1], 2)
     wait(rs_recv.at[pl.ds(0, PLANE - 1)], rs_sem.at[1])
     swap_w.start()
 
@@ -228,6 +232,8 @@
 
     lax.fori_loop(1, PLANE, ss_start, 0)
     ss_recv[me] = ss_send[...]
+    pl.semaphore_wait(near_sem.at[1], 2)
+    greet_z(near_sem.at[2], 4)
     wait(ss_recv.at[pl.ds(0, PLANE - 1)], ss_sem.at[1])
     sums = ss_recv[0]
     for j in range(1, PLANE):
@@ -299,8 +305,19 @@
                 plane_step(1 - order_of(n), 1 + 2 * i),
             )
 
+    def spread(n):
+        chunk = chunk_at(SEQ[n])
+
+        def step(i, carry):
+            j = lax.rem(x * Y + y + i, 16)
+            target = dev(lax.div(j, Y), lax.rem(j, Y), z, c)
+            send(chunk, chunk, ds_sem.at[0], p3_sem.at[n], target)
+            return carry
+
+        lax.fori_loop(1, 16, step, 0)
+
     def complete(n):
-        wait(xg.at[0, 0], p3_sem.at[n])
+        wait(xg.at[0, 0] if n < stepped else xg.at[pl.ds(0, 15), 0, 0], p3_sem.at[n])
         if SEQ[n] in GIFTS:
             step, index = GIFTS[SEQ[n]]
             whole = xg.at[zmate(SEQ[n])]
@@ -364,16 +381,23 @@
                 quant[r, zi] = packed[16 * r : 16 * r + 16]
 
     count = len(SEQ)
+    stepped = count - DIRECT
+    pl.semaphore_wait(near_sem.at[2], 2)
+    for n in range(1, 1 + AHEAD):
+        z_start(n)
     across(0)
-    for n in range(1, count):
-        z_start(n)
     for step in range(1, count + 2 * LAG + DONE):
+        if step + AHEAD < count:
+            z_start(step + AHEAD)
         if step < count:
             wait(mine, z_sem.at[step])
-            across(step)
-        if LAG <= step < count + LAG:
+            if step < stepped:
+                across(step)
+            else:
+                spread(step)
+        if LAG <= step < stepped + LAG:
             along(step - LAG)
-        if 2 * LAG <= step < count + 2 * LAG:
+        if 2 * LAG <= step < stepped + 2 * LAG:
             onward(step - 2 * LAG)
         if 2 * LAG + DONE <= step:
             complete(step - 2 * LAG - DONE)
@@ -453,12 +477,19 @@
         picks = jnp.sum(picks, axis=0, keepdims=True)
         pk_send[2 * r : 2 * r + 1] = picks[:, 0:128]
         pk_send[2 * r + 1 : 2 * r + 2] = picks[:, 128:256]
-    plane_start(pk_send, pk_plane, kp_sem)
+
+    def pk_start(i, carry):
+        j = lax.rem(me + i, PLANE)
+        send(pk_send, pk_plane.at[me], kp_sem.at[0], kp_sem.at[1], plane_dev(j))
+        return carry
+
+    lax.fori_loop(1, PLANE, pk_start, 0)
+    pk_plane[me] = pk_send[...]
 
     wait(st_plane.at[pl.ds(0, 15)], sp_sem.at[1])
     st_mid[...] = merge(st_plane)
     line_start(st_mid, st_z, sz_sem)
-    wait(pk_plane.at[pl.ds(0, 15)], kp_sem.at[1])
+    wait(pk_plane.at[pl.ds(0, PLANE - 1)], kp_sem.at[1])
     pk_mid[...] = jnp.sum(pk_plane[...], axis=0)
     line_start(pk_mid, pk_z, kz_sem)
 
@@ -482,16 +513,12 @@
     for r in range(ROUNDS):
         part = lf[r, :, :, other].reshape(128, COLS) - columns[:, r : r + 1]
         psend[r] = jnp.exp(part).astype(BF16).reshape(8, 16, COLS)
-    send(
-        psend, prob.at[:, :, c], pr_sem.at[0], pr_sem.at[1], dev(x, y, z, sib)
-    )
+        send(
+            psend.at[r], prob.at[r, :, c], pr_sem.at[0], pr_sem.at[1], dev(x, y, z, sib)
+        )
     for r in range(ROUNDS):
         part = lf[r, :, :, ours].reshape(128, COLS) - columns[:, r : r + 1]
         prob[r, :, c] = jnp.exp(part).astype(BF16).reshape(8, 16, COLS)
-
-    wait(pk_z.at[pl.ds(0, 15)], kz_sem.at[1])
-    pk_own[...] = jnp.sum(pk_z[...], axis=0)
-    send(pk_own, pk_sib, kb_sem.at[0], kb_sem.at[1], dev(x, y, z, sib))
 
     wait(st_sib, sb_sem.at[1])
     even = jnp.where(c == 0, st_own[...], st_sib[...])
@@ -515,9 +542,8 @@
     in_tree = (lax.div(iota((256, 128), 0), NODES) == lax.rem(lane, 4)).astype(F32)
     counted = dot(survive.astype(F32), in_tree, HIGHEST)
 
-    wait(pk_sib, kb_sem.at[1])
-    picks = jnp.where(c == 0, pk_own[...], pk_sib[...])
-    picks = picks + jnp.where(c == 0, pk_sib[...], pk_own[...])
+    wait(pk_z.at[pl.ds(0, 15)], kz_sem.at[1])
+    picks = jnp.sum(pk_z[...], axis=0)
     picked = jnp.concatenate(
         [
             jnp.concatenate([picks[2 * r : 2 * r + 1], picks[2 * r + 1 : 2 * r + 2]], axis=1)
@@ -534,18 +560,19 @@
 
     wait(prob.at[:, :, 0], pr_sem.at[1])
     wait(psend, pr_sem.at[0])
-    wait(pk_own, kb_sem.at[0])
     wait(st_own, sb_sem.at[0])
     wait(pk_z.at[pl.ds(0, 15)], kz_sem.at[0])
     wait(st_z.at[pl.ds(0, 15)], sz_sem.at[0])
-    wait(pk_plane.at[pl.ds(0, 15)], kp_sem.at[0])
+    wait(pk_plane.at[pl.ds(0, PLANE - 1)], kp_sem.at[0])
     wait(st_plane.at[pl.ds(0, 15)], sp_sem.at[0])
     wait(lr, ls_sem.at[0])
     if GIFTS:
         wait(xg.at[pl.ds(0, len(GIFTS))], gs_sem.at[0])
-    wait(xg.at[pl.ds(0, count), 0], p3s_sem.at[0])
-    wait(xg.at[pl.ds(0, count), pl.ds(0, 2)], p2s_sem.at[0])
-    wait(xg.at[pl.ds(0, count), 0, pl.ds(0, 3)], p1s_sem.at[0])
+    if DIRECT:
+        wait(xg.at[pl.ds(0, 15), 0, pl.ds(0, DIRECT)], ds_sem.at[0])
+    wait(xg.at[pl.ds(0, stepped), 0], p3s_sem.at[0])
+    wait(xg.at[pl.ds(0, stepped), pl.ds(0, 2)], p2s_sem.at[0])
+    wait(xg.at[pl.ds(0, stepped), 0, pl.ds(0, 3)], p1s_sem.at[0])
     wait(xg.at[pl.ds(0, count - 1), 0, 0], zs_sem.at[0])
     wait(ss_recv.at[pl.ds(0, PLANE - 1)], ss_sem.at[0])
     wait(rs_recv.at[pl.ds(0, PLANE - 1)], rs_sem.at[0])
@@ -589,11 +616,9 @@
             tile,
             tile,
             tile,
-            tiles,
+            pltpu.VMEM((PLANE, 8, 128), F32),
             tile,
             tiles,
-            tile,
-            tile,
             pltpu.VMEM((ROUNDS, 8, 16, COLS), BF16),
             pltpu.SemaphoreType.DMA((5,)),
             pltpu.SemaphoreType.DMA((3,)),
@@ -609,6 +634,7 @@
             one,
             pltpu.SemaphoreType.DMA((4,)),
             one,
+            one,
             pltpu.SemaphoreType.DMA((4,)),
             one,
             two,
@@ -617,7 +643,7 @@
             two,
             two,
             two,
-            two,
+            pltpu.SemaphoreType.REGULAR((3,)),
         ],
         compiler_params=pltpu.CompilerParams(
             collective_id=0, has_side_effects=True, vmem_limit_bytes=40 * 2**20

time: 78.8 us -> 75.1 us (0.953)
  Pallas kernels: 76.1 us -> 72.3 us
    pallas_call x1, Pallas kernels: 76.1 us -> 72.3 us  [body(): pl.pallas_call(kernel, out_shape=(jax.ShapeDtypeStruct((ROUNDS, 8, 2, 16,...]
where the time goes in v3:
time: 75.1 us; the launch traced here: 74.9 us
  Pallas kernels  72.3 us (96%)
  local copies, waits for them, and re-layouts  1.93 us (3%)
    pallas_call x1, Pallas kernels, body(): pl.pallas_call(kernel, out_shape=(jax.ShapeDtypeStruct((ROUNDS, 8, 2, 16,...  72.3 us

profile of v3, /device:TPU:1, one launch (start us, length us, event | category | flops | bytes accessed | tf_op | source)
XLA Modules:
  0.0 74.9 jit_solution(12190360832618788293)
XLA Ops:
  0.6 72.3 %verify.1 = (bf16[3,8,2,16,256]{4,3,2,1,0:T(8,128)(2,1)S(1)}, f32[16,256]{1,0:T(8,128)S(1)}) custom-call(bf16[3,1,4,4096]{3,2,1,0:T(4,128)(2,1)} %partials.1, bf16[4096]{0:T(1024)(128)(2,1)} %gain.1, bf16[4096,256]{1,0:T(8,128)(2,1)} %weight.1, s32[3,256]{1,0:T(4,128)} %draft_in.1, s32[1,256]{1,0:T(1,128)} %bitcast.3, s32[3,4]{1,0:T(4,128)} %accepted_in.1), custom_call_target="tpu_custom_call" | custom-call | tf_op jit(solution)/shard_map/verify/pallas_call | solution.py:588
  73.0 0.6 fusion
  73.6 0.6 slice.11
  74.2 0.7 copy.11

commit v4 on v3

--- a/solution.py
+++ b/solution.py
@@ -23,14 +23,14 @@
 SEQ = (0, 1, -1, 3, -3, 5, -5, 4, -4, 7, -7, 8)
 GIFTS = {1: (-1, 0), -1: (1, 1), 5: (-1, 2), -5: (1, 3)}
 GIVEN = {2: 0, -2: 1, 6: 2, -6: 3}
-GROUPS = ((0, 1, -1, 4), (2, 3, -3, -2), (-4, 5, -5, 8), (6, 7, -7, -6))
+GROUPS = ((0, 1, -1, 2), (-2, 3, -3, 4), (-4, 5, -5, 6), (8, 7, -7, -6))
 position = {o: n for n, o in enumerate(SEQ)}
 position.update({2: 1, -2: 2, 6: 5, -6: 6})
 LAG = 3
-DONE = 2
+DONE = 3
 AHEAD = 11
 DIRECT = 0
-HEADS = ((3, 0, 1), (5, 1, 2), (99, 2, 3), (99, 3, 4))
+HEADS = ((4, 0, 1), (6, 1, 2), (99, 2, 3), (99, 3, 4))
 norm_eps = 1e-06
 typical_alpha = 0.3
 

time: 75.1 us -> 73.3 us (0.976)
  Pallas kernels: 72.3 us -> 70.6 us
    pallas_call x1, Pallas kernels: 72.3 us -> 70.6 us  [body(): pl.pallas_call(kernel, out_shape=(jax.ShapeDtypeStruct((ROUNDS, 8, 2, 16,...]
where the time goes in v4:
time: 73.3 us; the launch traced here: 73.1 us
  Pallas kernels  70.6 us (96%)
  local copies, waits for them, and re-layouts  1.93 us (3%)
    pallas_call x1, Pallas kernels, body(): pl.pallas_call(kernel, out_shape=(jax.ShapeDtypeStruct((ROUNDS, 8, 2, 16,...  70.6 us

profile of v4, /device:TPU:1, one launch (start us, length us, event | category | flops | bytes accessed | tf_op | source)
XLA Modules:
  0.0 73.1 jit_solution(7552671816722140689)
XLA Ops:
  0.6 70.6 %verify.1 = (bf16[3,8,2,16,256]{4,3,2,1,0:T(8,128)(2,1)S(1)}, f32[16,256]{1,0:T(8,128)S(1)}) custom-call(bf16[3,1,4,4096]{3,2,1,0:T(4,128)(2,1)} %partials.1, bf16[4096]{0:T(1024)(128)(2,1)} %gain.1, bf16[4096,256]{1,0:T(8,128)(2,1)} %weight.1, s32[3,256]{1,0:T(4,128)} %draft_in.1, s32[1,256]{1,0:T(1,128)} %bitcast.3, s32[3,4]{1,0:T(4,128)} %accepted_in.1), custom_call_target="tpu_custom_call" | custom-call | tf_op jit(solution)/shard_map/verify/pallas_call | solution.py:588
  71.2 0.6 fusion
  71.8 0.6 slice.11
  72.4 0.7 %copy.11 = bf16[3,256,256]{2,1,0:T(8,128)(2,1)} copy(bf16[3,256,256]{2,1,0:T(8,128)(2,1)S(1)} %bitcast.2) | data formatting | bytes 786432

commit v5 on v4

--- a/solution.py
+++ b/solution.py
@@ -31,6 +31,10 @@
 AHEAD = 11
 DIRECT = 0
 HEADS = ((4, 0, 1), (6, 1, 2), (99, 2, 3), (99, 3, 4))
+FAR_FIRST = sorted(
+    ((dx, dy) for dx in range(X) for dy in range(Y) if dx or dy),
+    key=lambda o: abs(o[0] - 2) + abs(o[1] - 2),
+)
 norm_eps = 1e-06
 typical_alpha = 0.3
 
@@ -188,12 +192,13 @@
     pl.semaphore_wait(barrier, PLANE - 1 + 2)
     greet_z(near_sem.at[0], 1)
 
-    def rs_start(i, carry):
-        j = lax.rem(me + i, PLANE)
-        send(rs_send.at[j], rs_recv.at[me], rs_sem.at[0], rs_sem.at[1], plane_dev(j))
-        return carry
-
-    lax.fori_loop(1, PLANE, rs_start, 0)
+    others = []
+    for dx, dy in FAR_FIRST + [(0, 0)]:
+        nx, ny = lax.rem(x + dx, X), lax.rem(y + dy, Y)
+        for nc in (c, sib)[0 if dx or dy else 1 :]:
+            others.append((nc * 16 + nx * Y + ny, dev(nx, ny, z, nc)))
+    for j, target in others:
+        send(rs_send.at[j], rs_recv.at[me], rs_sem.at[0], rs_sem.at[1], target)
     rs_recv[me] = rs_send[me]
 
     swap_w = pltpu.make_async_remote_copy(
@@ -225,12 +230,8 @@
         jnp.sum(square.T, axis=0, keepdims=True), (8, 128)
     )
 
-    def ss_start(i, carry):
-        j = lax.rem(me + i, PLANE)
-        send(ss_send, ss_recv.at[me], ss_sem.at[0], ss_sem.at[1], plane_dev(j))
-        return carry
-
-    lax.fori_loop(1, PLANE, ss_start, 0)
+    for j, target in others:
+        send(ss_send, ss_recv.at[me], ss_sem.at[0], ss_sem.at[1], target)
     ss_recv[me] = ss_send[...]
     pl.semaphore_wait(near_sem.at[1], 2)
     greet_z(near_sem.at[2], 4)
@@ -407,38 +408,23 @@
         for at, first, last in HEADS:
             if step == at + count:
                 head(first, last)
-    ready = 0
     for at, first, last in HEADS:
-        if at + count >= count + 2 * LAG + DONE:
+        if at >= 2 * LAG + DONE:
             head(first, last)
-            for g in range(ready, last - 1):
-                stats(g)
-            ready = last - 1
-    stats(len(GROUPS) - 1)
+    for g in range(len(GROUPS)):
+        stats(g)
 
     chip = x * Y + y
 
     def plane_start(src, dst, sems):
-        def step(i, carry):
-            j = lax.rem(chip + i, 16)
-            send(
-                src,
-                dst.at[chip],
-                sems.at[0],
-                sems.at[1],
-                dev(lax.div(j, Y), lax.rem(j, Y), z, c),
-            )
-            return carry
-
-        lax.fori_loop(1, 16, step, 0)
+        for dx, dy in FAR_FIRST:
+            target = dev(lax.rem(x + dx, X), lax.rem(y + dy, Y), z, c)
+            send(src, dst.at[chip], sems.at[0], sems.at[1], target)
         dst[chip] = src[...]
 
     def line_start(src, dst, sems):
-        def step(i, carry):
-            send(src, dst.at[z], sems.at[0], sems.at[1], dev(x, y, zmate(i), c))
-            return carry
-
-        lax.fori_loop(1, Z, step, 0)
+        for o in sorted(range(1, Z), key=lambda o: abs(o - 8)):
+            send(src, dst.at[z], sems.at[0], sems.at[1], dev(x, y, zmate(o), c))
         dst[z] = src[...]
 
     def merge(ref):

time: 73.3 us -> 72.6 us (level)
  no operation moved by 1% of the time
where the time goes in v5:
time: 72.6 us; the launch traced here: 72.4 us
  Pallas kernels  69.9 us (96%)
  local copies, waits for them, and re-layouts  1.93 us (3%)
    pallas_call x1, Pallas kernels, body(): pl.pallas_call(kernel, out_shape=(jax.ShapeDtypeStruct((ROUNDS, 8, 2, 16,...  69.9 us

profile of v5, /device:TPU:1, one launch (start us, length us, event | category | flops | bytes accessed | tf_op | source)
XLA Modules:
  0.0 72.4 jit_solution(16327333255409452458)
XLA Ops:
  0.6 69.9 %verify.1 = (bf16[3,8,2,16,256]{4,3,2,1,0:T(8,128)(2,1)S(1)}, f32[16,256]{1,0:T(8,128)S(1)}) custom-call(bf16[3,1,4,4096]{3,2,1,0:T(4,128)(2,1)} %partials.1, bf16[4096]{0:T(1024)(128)(2,1)} %gain.1, bf16[4096,256]{1,0:T(8,128)(2,1)} %weight.1, s32[3,256]{1,0:T(4,128)} %draft_in.1, s32[1,256]{1,0:T(1,128)} %bitcast.3, s32[3,4]{1,0:T(4,128)} %accepted_in.1), custom_call_target="tpu_custom_call" | custom-call | tf_op jit(solution)/shard_map/verify/pallas_call | solution.py:574
  70.5 0.6 fusion
  71.1 0.6 slice.11
  71.7 0.7 %copy.11 = bf16[3,256,256]{2,1,0:T(8,128)(2,1)} copy(bf16[3,256,256]{2,1,0:T(8,128)(2,1)S(1)} %bitcast.2) | data formatting | bytes 786432
